TPU v7x, 128 devices: a whole 4x4x4 slice. The times are simulated.
128 devices in a mesh: ba: 8 (over z, core), bb: 16 (over y, x).
Axes of the slice: x: 4, y: 4, z: 4, core: 2. Of those that a mesh axis runs over, the one named last changes fastest.
Arguments:
- tensor: bfloat16 [2, 64, 5, 384, 384], P(None, 'ba', None, 'bb'), may hold values from -6 to 6
- occupied: bfloat16 [64, 3, 384, 384], P('ba', None, 'bb'), may hold values from -0.1875 to 0.1875
- virtual: bfloat16 [64, 3, 384, 384], P('ba', None, 'bb'), may hold values from -0.1875 to 0.1875
- tensor_mask: int32 [64, 5], replicated, may hold values 0 or 1
- occupied_mask: int32 [64, 3], replicated, may hold values 0 or 1
- virtual_mask: int32 [64, 3], replicated, may hold values 0 or 1
Outputs:
- product_slab: bfloat16 [2, 64, 5, 384, 384], P(None, 'ba', None, 'bb')
- coupling: float32 [2, 2], replicated
All inputs are finite; a program needn't handle non-finite values.
Results may differ from a plain program's by a relative error of at most 0.0067.
Values may be sent and summed in bfloat16 or wider, within the bound.
A program may use at most 128 MiB of HBM per device.

v0:
```python
import math

import jax
import jax.numpy as jnp
from jax import lax
from jax.experimental import pallas as pl
from jax.experimental.pallas import tpu as pltpu
from jax.sharding import PartitionSpec as P

BASIS = 24576
BLK = 384
HB = 5
MESH = pl.DeviceIdType.MESH
VMEM_LIMIT = 56 * 1024 * 1024

ROWS = 24
T_ROWS = 128
V_ROWS = 80
O_ROWS = 144
E_ROWS = 32
O_SPAN = ((16, 128), (0, 144), (0, 128))

ORDER = (
    (0, 0), (2, 2), (1, 0), (0, 1), (3, 0), (0, 3), (1, 1), (3, 3),
    (1, 3), (3, 1), (2, 0), (0, 2), (2, 1), (1, 2), (2, 3), (3, 2),
)


def pick(table, index):
    value = 0
    for position, entry in enumerate(table):
        if entry:
            value = value + jnp.where(index == position, entry, 0)
    return value


def chip_of(p, j):
    x = jnp.where(j < 4, j, 7 - j)
    y = jnp.where(j < 4, p, 3 - p)
    return y * 4 + x


def work_of(chip):
    x, y = chip % 4, chip // 4
    upper = y >= 2
    j = jnp.where(upper, 7 - x, x)
    p = jnp.where(upper, 3 - y, y)
    return p, j


def target_chip(step, chip, core):
    dx, dy = pick([d[0] for d in ORDER], step), pick([d[1] for d in ORDER], step)
    ex = jnp.where(core == 0, dx, dy)
    ey = jnp.where(core == 0, dy, dx)
    return ((chip // 4 + ey) % 4) * 4 + (chip % 4 + ex) % 4


def place():
    a, chip = lax.axis_index("ba"), lax.axis_index("bb")
    return a, chip, a // 2, a % 2


def greet(bar, a, b):
    pl.semaphore_signal(bar, inc=1, device_id=(a, b), device_id_type=MESH)


def plane_barrier(bar, a, z, chip):
    def hello(k, carry):
        other_a, other_chip = 2 * z + k // 16, k % 16

        @pl.when(jnp.logical_not((other_a == a) & (other_chip == chip)))
        def _():
            greet(bar, other_a, other_chip)

        return carry

    lax.fori_loop(0, 32, hello, 0)


def drain(count, ref, sem):
    def one(k, carry):
        pltpu.make_async_copy(ref, ref, sem).wait()
        return carry

    lax.fori_loop(0, count, one, 0)


def send(cond, is_self, src, dst, send_sem, recv_sem, device):
    @pl.when(cond & is_self)
    def _():
        pltpu.make_async_copy(src, dst, recv_sem).start()

    @pl.when(cond & jnp.logical_not(is_self))
    def _():
        pltpu.make_async_remote_copy(
            src_ref=src, dst_ref=dst, send_sem=send_sem, recv_sem=recv_sem,
            device_id=device, device_id_type=MESH,
        ).start()

    return jnp.where(cond & jnp.logical_not(is_self), 1, 0)


def source_row(p, core):
    return jnp.where(p == 0, 3 * core, 1 + core)


def rpa_kernel(
    tm_ref, om_ref, vm_ref, t_ref, v_ref, o_ref, y_ref, c_ref,
    tr, vr, oc, er, t_loc, tc, vv, col, w, prod, y_send, slots, held, slots2,
    loc_sem, t_send, t_recv, v_send, v_recv, o_send, o_recv, e_send, e_recv,
    f_send, f_recv, h_send, h_recv, g_send, g_recv, i_send, i_recv,
    y_out, y_in, s_send, s_recv, s_send2, s_recv2,
):
    f32, bf = jnp.float32, jnp.bfloat16
    a, chip, z, core = place()
    p_me, j_me = work_of(chip)
    s_me = 16 * z + 2 * j_me + core
    bar = pltpu.get_barrier_semaphore()
    plane_barrier(bar, a, z, chip)

    def hello_group(k, carry):
        greet(bar, (2 * z + 2 + k) % 8, chip)
        return carry

    lax.fori_loop(0, 6, hello_group, 0)

    @pl.when(j_me < 2)
    def _():
        def hello(k, carry):
            greet(bar, (2 * z + 7) % 8, k)
            return carry

        lax.fori_loop(0, 16, hello, 0)

    @pl.when(j_me >= 6)
    def _():
        def hello(k, carry):
            greet(bar, (2 * z + 2) % 8, k)
            return carry

        lax.fori_loop(0, 16, hello, 0)

    t_copy = pltpu.make_async_copy(t_ref, t_loc, loc_sem)
    t_copy.start()

    up_z = jnp.where(s_me % 16 < 15, z, (z + 1) % 4)
    up_j = jnp.where(core == 0, j_me, (j_me + 1) % 8)
    down_z = jnp.where(s_me % 16 > 0, z, (z + 3) % 4)
    down_j = jnp.where(core == 1, j_me, (j_me + 7) % 8)
    up = (2 * up_z + 1 - core, chip_of(p_me, up_j))
    down = (2 * down_z + 1 - core, chip_of(p_me, down_j))
    twin = (2 * z + 1 - core, chip)
    partner = (a, chip_of(1 - p_me, j_me))

    pl.semaphore_wait(bar, 45)

    y_me = chip // 4
    p_want = jnp.where((y_me == 0) | (y_me == 3), 0, 1)
    core_want = jnp.where(y_me < 2, 0, 1)

    def planes(j):
        outer_z = jnp.where(core == 0, (z + 3) % 4, (z + 1) % 4)
        return ((j, z, True), (j + jnp.where(core == 0, -8, 8), outer_z, False))

    def send_occ(step, counts):
        counts = list(counts)
        chip_to = target_chip(step, chip, core)
        p, j = work_of(chip_to)
        for j_rel, to_z, inside in planes(j):
            for kind in range(3):
                first, rows = O_SPAN[kind]
                ml = j_rel + kind - 1 - 4 * core
                hit = (ml >= 0) & (ml < 4) & (p == p_want)
                ml = jnp.where(hit, ml, 0)
                own = (chip_to == chip) & (core == core_want)
                counts[kind] = counts[kind] + send(
                    hit, own if inside else (own & False),
                    o_ref.at[ml, pl.ds(first, rows)],
                    oc.at[kind, chip, pl.ds(first, rows)],
                    o_send.at[kind], o_recv.at[kind],
                    (2 * to_z + core_want, chip_to),
                )
        return tuple(counts)

    o_counts = lax.fori_loop(0, 16, send_occ, (0, 0, 0))

    def send_t(step, count):
        chip_to = target_chip(step, chip, core)
        p, j = work_of(chip_to)
        mine = j // 4 == core
        pair = jnp.where(mine, j - 4 * core, 0)
        for half in range(2):
            count = count + send(
                mine, (chip_to == chip) & (core == half),
                t_ref.at[p, pair, pl.ds(112 * half, T_ROWS)], tr.at[1, chip], t_send, t_recv,
                (2 * z + half, chip_to),
            )
        return count

    t_count = lax.fori_loop(0, 16, send_t, 0)

    def part(kind, row):
        first, rows = O_SPAN[kind]
        return oc.at[kind, pl.ds(4 * row, 4), pl.ds(first, rows)]

    def hand_on(kind, row, device, send_sem, recv_sem):
        copy = pltpu.make_async_remote_copy(
            src_ref=part(kind, row), dst_ref=part(kind, row),
            send_sem=send_sem.at[kind], recv_sem=recv_sem.at[kind],
            device_id=device, device_id_type=MESH,
        )
        copy.start()
        return copy

    def arrived(ref, sem):
        pltpu.make_async_copy(ref, ref, sem).wait()

    copies = []
    for kind in range(3):
        row = source_row(p_me, core)
        arrived(part(kind, row), o_recv.at[kind])
        copies.append(hand_on(kind, row, partner, g_send, g_recv))
        copies.append(hand_on(kind, row, twin, h_send, h_recv))

    arrived(tr.at[1], t_recv)
    for slot, device in ((2, down), (0, up)):
        copy = pltpu.make_async_remote_copy(
            src_ref=tr.at[1], dst_ref=tr.at[slot],
            send_sem=f_send.at[slot // 2], recv_sem=f_recv.at[slot // 2],
            device_id=device, device_id_type=MESH,
        )
        copy.start()
        copies.append(copy)

    def send_rest(step, counts):
        v_count, e_count = counts
        chip_to = target_chip(step, chip, core)
        p, j = work_of(chip_to)
        same = chip_to == chip
        mine = j // 4 == core
        pair = jnp.where(mine, j - 4 * core, 0)
        for half in range(2):
            v_count = v_count + send(
                mine, same & (core == half),
                v_ref.at[pair, pl.ds(64 * half, V_ROWS)], vr.at[chip], v_send, v_recv,
                (2 * z + half, chip_to),
            )
        for j_rel, to_z, inside in planes(j):
            for to_core, first, kind in ((0, 112, -2), (1, 0, 2)):
                ml = j_rel + kind - 4 * core
                hit = (ml >= 0) & (ml < 4)
                ml = jnp.where(hit, ml, 0)
                own = same & (core == to_core)
                e_count = e_count + send(
                    hit, own if inside else (own & False),
                    o_ref.at[ml, pl.ds(first, E_ROWS)], er.at[chip], e_send, e_recv,
                    (2 * to_z + to_core, chip_to),
                )
        return v_count, e_count

    v_count, e_count = lax.fori_loop(0, 16, send_rest, (0, 0))

    for kind in range(3):
        row = source_row(1 - p_me, core)
        arrived(part(kind, row), g_recv.at[kind])
        copies.append(hand_on(kind, row, twin, i_send, i_recv))

    def joined(low, high, row, factor):
        both = jnp.concatenate([low[row : row + ROWS], high[row : row + ROWS]], axis=0)
        return (both * factor).astype(bf)

    def window(q):
        return pl.ds(pl.multiple_of(q * 2 * ROWS, 16), 2 * ROWS)

    def flag(ref, block, entry):
        return ref[(block + 64) % 64, entry].astype(f32)

    def shifted(ref, odd, rows):
        full = ref.astype(f32)
        return jnp.where(odd, full[8 : 8 + rows], full[:rows])

    def spread_t(g):
        factors = [flag(tm_ref, s_me + g - 1, h) for h in range(HB)]
        odd = (core == 1) if g == 1 else (core == 0)

        def one(q, carry):
            low = shifted(tr[g, 2 * q], odd, 120)
            high = shifted(tr[g, 2 * q + 1], odd, 120)
            for h in range(HB):
                tc[g, window(q), h * BLK : (h + 1) * BLK] = joined(low, high, h * ROWS, factors[h])
            return carry

        lax.fori_loop(0, 8, one, 0)

    spread_t(1)

    arrived(vr, v_recv)
    v_factors = [flag(vm_ref, s_me, g) for g in range(3)]

    def spread_v(q, carry):
        low = shifted(vr[2 * q], core == 1, 72)
        high = shifted(vr[2 * q + 1], core == 1, 72)
        for g in range(3):
            vv[g, window(q), :] = joined(low, high, g * ROWS, v_factors[g])
        return carry

    lax.fori_loop(0, 8, spread_v, 0)

    arrived(er, e_recv)
    edge_block = jnp.where(core == 0, s_me - 3, s_me + 3)
    edge_factor = jnp.where(core == 0, flag(om_ref, edge_block, 2), flag(om_ref, edge_block, 0))

    def spread_e(q, carry):
        low, high = er[2 * q].astype(f32), er[2 * q + 1].astype(f32)

        @pl.when(core == 0)
        def _():
            col[0, window(q), :] = joined(low, high, 8, edge_factor)

        @pl.when(core == 1)
        def _():
            at = pl.ds(pl.multiple_of(2 * BLK + q * 2 * ROWS, 16), 2 * ROWS)
            col[5, at, :] = joined(low, high, 0, edge_factor)

        return carry

    lax.fori_loop(0, 8, spread_e, 0)

    for kind in range(3):
        arrived(part(kind, source_row(p_me, 1 - core)), h_recv.at[kind])
        arrived(part(kind, source_row(1 - p_me, 1 - core)), i_recv.at[kind])
        first, rows = O_SPAN[kind]
        wanted = [
            (k, g, 2 * kind + k + g - 1)
            for k in range(2) for g in range(3)
            if 0 <= 2 * kind + k + g - 1 < 6
        ]
        base = 16 * z + 2 * (j_me + kind - 1)
        factors = [flag(om_ref, base + k, g) for k, g, _ in wanted]

        def spread_o(q, carry):
            low = oc[kind, 2 * q, first : first + rows].astype(f32)
            high = oc[kind, 2 * q + 1, first : first + rows].astype(f32)
            for (k, g, column), factor in zip(wanted, factors):
                at = pl.ds(pl.multiple_of((2 - g) * BLK + q * 2 * ROWS, 16), 2 * ROWS)
                col[column, at, :] = joined(low, high, (3 * k + g) * ROWS - first, factor)
            return carry

        lax.fori_loop(0, 8, spread_o, 0)

    for slot in (0, 2):
        arrived(tr.at[slot], f_recv.at[slot // 2])
        spread_t(slot)

    for o in range(7):
        total = None
        for g in range(3):
            h = o - g
            if 0 <= h < HB:
                term = jnp.dot(
                    vv[g], tc[g, :, h * BLK : (h + 1) * BLK], preferred_element_type=f32
                )
                total = term if total is None else total + term
        w[:, o * BLK : (o + 1) * BLK] = total.astype(bf)
    for h in range(HB):
        block = jnp.dot(
            w[:, h * BLK : (h + 3) * BLK], col[core + h], preferred_element_type=f32
        )
        prod[h] = block * flag(tm_ref, s_me, h)

    to_core = j_me // 4
    il_me = 2 * (j_me % 4) + core

    def regroup(step, count):
        chip_to = target_chip(step, chip, core)
        rows = pl.ds(pl.multiple_of(chip_to * ROWS, 8), ROWS)
        pieces = [prod[h, rows, :] for h in range(HB)]
        pieces.append(jnp.zeros((T_ROWS - HB * ROWS, BLK), f32))
        y_send[chip_to] = jnp.concatenate(pieces, axis=0).astype(bf)
        return count + send(
            chip_to >= 0, (chip_to == chip) & (to_core == core),
            y_send.at[chip_to], y_ref.at[p_me, il_me], y_out, y_in,
            (2 * z + to_core, chip_to),
        )

    y_count = lax.fori_loop(0, 16, regroup, 0)

    for copy in copies:
        copy.wait_send()
    drain(t_count, t_ref.at[0, 0, pl.ds(0, T_ROWS)], t_send)
    drain(v_count, v_ref.at[0, pl.ds(0, V_ROWS)], v_send)
    drain(e_count, o_ref.at[0, pl.ds(0, E_ROWS)], e_send)
    for kind, count in enumerate(o_counts):
        drain(count, o_ref.at[0, pl.ds(0, O_SPAN[kind][1])], o_send.at[kind])
    t_copy.wait()

    arrived(y_ref, y_in)

    def couple(pair, sums):
        sums = list(sums)
        ts = [t_loc[q, pair].astype(f32) for q in range(2)]
        for p in range(2):
            for half in range(2):
                y = y_ref[p, 2 * pair + half].astype(f32)[: HB * ROWS]
                for q in range(2):
                    both = y * ts[q][half * HB * ROWS : (half + 1) * HB * ROWS]
                    both = jnp.sum(both.reshape(HB * ROWS // 8, 8, BLK), axis=0)
                    sums[2 * p + q] = sums[2 * p + q] + both
        return tuple(sums)

    sums = lax.fori_loop(0, 4, couple, (jnp.zeros((8, BLK), f32),) * 4)
    lane = lax.broadcasted_iota(jnp.int32, (8, 128), 1)
    mine = jnp.zeros((8, 128), f32)
    for k in range(4):
        part_sum = sums[k][:, :128] + sums[k][:, 128:256] + sums[k][:, 256:]
        column = jnp.sum(part_sum, axis=1, keepdims=True)
        mine = mine + jnp.where(lane == k, column, 0.0)
    held[0] = mine
    slots[chip] = mine

    def to_chip(k, carry):
        pltpu.make_async_remote_copy(
            src_ref=held.at[0], dst_ref=slots.at[chip], send_sem=s_send, recv_sem=s_recv,
            device_id=(a, (chip + k) % 16), device_id_type=MESH,
        ).start()
        return carry

    lax.fori_loop(1, 16, to_chip, 0)
    most = slots.at[pl.ds(0, 15)]
    arrived(most, s_recv)
    total = slots[0]
    for k in range(1, 16):
        total = total + slots[k]
    held[1] = total
    slots2[a] = total

    def to_group(k, carry):
        pltpu.make_async_remote_copy(
            src_ref=held.at[1], dst_ref=slots2.at[a], send_sem=s_send2, recv_sem=s_recv2,
            device_id=((a + k) % 8, chip), device_id_type=MESH,
        ).start()
        return carry

    lax.fori_loop(1, 8, to_group, 0)
    most2 = slots2.at[pl.ds(0, 7)]
    arrived(most2, s_recv2)
    total = slots2[0]
    for k in range(1, 8):
        total = total + slots2[k]
    total = jnp.sum(total, axis=0, keepdims=True)
    c_ref[...] = jnp.broadcast_to(total, (8, 128)) / math.sqrt(BASIS * HB * BLK)
    arrived(most, s_send)
    arrived(most2, s_send2)
    drain(y_count, y_send.at[0], y_out)


def shards(tensor, occupied, virtual, tensor_mask, occupied_mask, virtual_mask):
    f32, bf = jnp.float32, jnp.bfloat16
    dma = pltpu.SemaphoreType.DMA
    vmem = pl.BlockSpec(memory_space=pltpu.VMEM)
    smem = pl.BlockSpec(memory_space=pltpu.SMEM)
    anywhere = pl.BlockSpec(memory_space=pl.ANY)
    product, coupling = pl.pallas_call(
        rpa_kernel,
        out_shape=(
            jax.ShapeDtypeStruct((2, 8, T_ROWS, BLK), bf),
            jax.ShapeDtypeStruct((8, 128), f32),
        ),
        in_specs=[smem] * 3 + [anywhere] * 3,
        out_specs=(vmem, vmem),
        scratch_shapes=[
            pltpu.VMEM((3, 16, T_ROWS, BLK), bf),
            pltpu.VMEM((16, V_ROWS, BLK), bf),
            pltpu.VMEM((3, 16, O_ROWS, BLK), bf),
            pltpu.VMEM((16, E_ROWS, BLK), bf),
            pltpu.VMEM((2, 4, 2 * HB * ROWS, BLK), bf),
            pltpu.VMEM((3, BLK, HB * BLK), bf),
            pltpu.VMEM((3, BLK, BLK), bf),
            pltpu.VMEM((6, 3 * BLK, BLK), bf),
            pltpu.VMEM((BLK, 7 * BLK), bf),
            pltpu.VMEM((HB, BLK, BLK), f32),
            pltpu.VMEM((16, T_ROWS, BLK), bf),
            pltpu.VMEM((16, 8, 128), f32),
            pltpu.VMEM((2, 8, 128), f32),
            pltpu.VMEM((8, 8, 128), f32),
            dma, dma, dma, dma, dma, dma((3,)), dma((3,)), dma, dma,
            dma((2,)), dma((2,)), dma((3,)), dma((3,)), dma((3,)), dma((3,)), dma((3,)), dma((3,)),
            dma, dma, dma, dma, dma, dma,
        ],
        compiler_params=pltpu.CompilerParams(
            collective_id=0, has_side_effects=True, vmem_limit_bytes=VMEM_LIMIT
        ),
        cost_estimate=pl.CostEstimate(
            flops=30 * 2 * BLK**3, bytes_accessed=20_000_000, transcendentals=0
        ),
        name="rpa_point",
    )(
        tensor_mask, occupied_mask, virtual_mask,
        tensor.reshape(2, 4, 2 * HB * ROWS, BLK),
        virtual.reshape(4, O_ROWS, BLK),
        occupied.reshape(4, O_ROWS, BLK),
    )
    rows = product[:, :, : HB * ROWS].reshape(2, 8, HB, ROWS, BLK)
    return (rows, coupling[0, :4].reshape(2, 2))


def solution(mesh):
    placed = (
        P(None, "ba", None, "bb", None),
        P("ba", None, "bb", None),
        P("ba", None, "bb", None),
        P(),
        P(),
        P(),
    )
    return jax.shard_map(
        shards,
        mesh=mesh,
        in_specs=placed,
        out_specs=(P(None, "ba", None, "bb", None), P()),
        check_vma=False,
    )
```

profile of v0, /device:TPU:1, one launch (start us, length us, event | category | flops | bytes accessed | tf_op | source)
XLA Modules:
  0.0 130.0 jit_solution(14252204546443824208)
XLA Ops:
  0.6 1.4 %copy.8.tm_ref = s32[64,5]{1,0:T(8,128)} copy(s32[64,5]{0,1:T(8,128)} %param.9) | data formatting | bytes 2560 | tf_op args[3]
  2.0 1.4 %copy.9.om_ref = s32[64,3]{1,0:T(8,128)} copy(s32[64,3]{0,1:T(4,128)} %param.10) | data formatting | bytes 1536 | tf_op args[4]
  3.4 1.4 %copy.10.vm_ref = s32[64,3]{1,0:T(8,128)} copy(s32[64,3]{0,1:T(4,128)} %param.11) | data formatting | bytes 1536 | tf_op args[5]
  4.8 121.3 %rpa_point.1 = (bf16[2,8,128,384]{3,2,1,0:T(8,128)(2,1)}, f32[8,128]{1,0:T(8,128)}) custom-call(s32[64,5]{1,0:T(8,128)} %copy.8.tm_ref, s32[64,3]{1,0:T(8,128)} %copy.9.om_ref, s32[64,3]{1,0:T(8,128)} %copy.10.vm_ref, bf16[2,4,240,384]{3,2,1,0:T(8,128)(2,1)} %bitcast.5, bf16[4,144,384]{2,1,0:T(8,128)(2,1)} %bitcast.6, bf16[4,144,384]{2,1,0:T(8,128)(2,1)} %bitcast.7), custom_call_target="tpu_custom_call" | custom-call | flops 3397386240 | bytes 20000000 | tf_op jit(solution)/shard_map/rpa_point/pallas_call | solution.py:463
  126.0 2.6 %slice.6 = bf16[2,8,120,384]{3,2,1,0:T(8,128)(2,1)} slice(bf16[2,8,128,384]{3,2,1,0:T(8,128)(2,1)} %get-tuple-element.4), slice={[0:2], [0:8], [0:120], [0:384]} | slice | bytes 2949120 | tf_op jit(solution)/shard_map/slice | solution.py:503
  128.7 0.7 slice_reduce_fusion
  129.4 0.6 reshape_squeeze.3
where the time goes:
time: 130 us
  Pallas kernels  121 us (93%)
  local copies, waits for them, and re-layouts  8.1 us (6%)
    pallas_call x1, Pallas kernels, shards(): pl.pallas_call(rpa_kernel, out_shape=(jax.ShapeDtypeStruct((2, 8, T_ROWS,...  121 us
    unnamed x3, local copies, waits for them, and re-layouts  4.12 us
    slice x1, local copies, waits for them, and re-layouts, shards(): rows = product[:, :, :HB * ROWS].reshape(2, 8, HB, ROWS, BLK)  2.64 us

commit v1 on v0

--- a/solution.py
+++ b/solution.py
@@ -64,17 +64,13 @@
     pl.semaphore_signal(bar, inc=1, device_id=(a, b), device_id_type=MESH)
 
 
-def plane_barrier(bar, a, z, chip):
-    def hello(k, carry):
-        other_a, other_chip = 2 * z + k // 16, k % 16
-
-        @pl.when(jnp.logical_not((other_a == a) & (other_chip == chip)))
+def plane_barrier(bar, a, core, chip):
+    for k in range(16):
+        greet(bar, a + 1 - 2 * core, k)
+
+        @pl.when(chip != k)
         def _():
-            greet(bar, other_a, other_chip)
-
-        return carry
-
-    lax.fori_loop(0, 32, hello, 0)
+            greet(bar, a, k)
 
 
 def drain(count, ref, sem):
@@ -105,8 +101,8 @@
 
 
 def rpa_kernel(
-    tm_ref, om_ref, vm_ref, t_ref, v_ref, o_ref, y_ref, c_ref,
-    tr, vr, oc, er, t_loc, tc, vv, col, w, prod, y_send, slots, held, slots2,
+    tm_ref, om_ref, vm_ref, t_ref, v_ref, o_ref, out_ref, c_ref,
+    y_ref, tr, vr, oc, er, t_loc, tc, vv, col, w, prod, y_send, slots, held, slots2,
     loc_sem, t_send, t_recv, v_send, v_recv, o_send, o_recv, e_send, e_recv,
     f_send, f_recv, h_send, h_recv, g_send, g_recv, i_send, i_recv,
     y_out, y_in, s_send, s_recv, s_send2, s_recv2,
@@ -116,29 +112,22 @@
     p_me, j_me = work_of(chip)
     s_me = 16 * z + 2 * j_me + core
     bar = pltpu.get_barrier_semaphore()
-    plane_barrier(bar, a, z, chip)
-
-    def hello_group(k, carry):
-        greet(bar, (2 * z + 2 + k) % 8, chip)
-        return carry
-
-    lax.fori_loop(0, 6, hello_group, 0)
+    plane_barrier(bar, a, core, chip)
+
+    z_up, z_down = (z + 1) % 4, (z + 3) % 4
+    for other_z in (z_up, z_down, (z + 2) % 4):
+        greet(bar, 2 * other_z, chip)
+        greet(bar, 2 * other_z + 1, chip)
 
     @pl.when(j_me < 2)
     def _():
-        def hello(k, carry):
-            greet(bar, (2 * z + 7) % 8, k)
-            return carry
-
-        lax.fori_loop(0, 16, hello, 0)
+        for k in range(16):
+            greet(bar, 2 * z_down + 1, k)
 
     @pl.when(j_me >= 6)
     def _():
-        def hello(k, carry):
-            greet(bar, (2 * z + 2) % 8, k)
-            return carry
-
-        lax.fori_loop(0, 16, hello, 0)
+        for k in range(16):
+            greet(bar, 2 * z_up, k)
 
     t_copy = pltpu.make_async_copy(t_ref, t_loc, loc_sem)
     t_copy.start()
@@ -177,7 +166,7 @@
                     hit, own if inside else (own & False),
                     o_ref.at[ml, pl.ds(first, rows)],
                     oc.at[kind, chip, pl.ds(first, rows)],
-                    o_send.at[kind], o_recv.at[kind],
+                    o_send.at[kind], o_recv.at[kind, chip % 4],
                     (2 * to_z + core_want, chip_to),
                 )
         return tuple(counts)
@@ -192,21 +181,20 @@
         for half in range(2):
             count = count + send(
                 mine, (chip_to == chip) & (core == half),
-                t_ref.at[p, pair, pl.ds(112 * half, T_ROWS)], tr.at[1, chip], t_send, t_recv,
+                t_ref.at[p, pair, pl.ds(112 * half, T_ROWS)], tr.at[1, chip], t_send, t_recv.at[chip // 4],
                 (2 * z + half, chip_to),
             )
         return count
 
     t_count = lax.fori_loop(0, 16, send_t, 0)
 
-    def part(kind, row):
+    def part(kind, start, count=4):
         first, rows = O_SPAN[kind]
-        return oc.at[kind, pl.ds(4 * row, 4), pl.ds(first, rows)]
-
-    def hand_on(kind, row, device, send_sem, recv_sem):
+        return oc.at[kind, pl.ds(start, count), pl.ds(first, rows)]
+
+    def hand_on(ref, device, send_sem, recv_sem):
         copy = pltpu.make_async_remote_copy(
-            src_ref=part(kind, row), dst_ref=part(kind, row),
-            send_sem=send_sem.at[kind], recv_sem=recv_sem.at[kind],
+            src_ref=ref, dst_ref=ref, send_sem=send_sem, recv_sem=recv_sem,
             device_id=device, device_id_type=MESH,
         )
         copy.start()
@@ -214,23 +202,6 @@
 
     def arrived(ref, sem):
         pltpu.make_async_copy(ref, ref, sem).wait()
-
-    copies = []
-    for kind in range(3):
-        row = source_row(p_me, core)
-        arrived(part(kind, row), o_recv.at[kind])
-        copies.append(hand_on(kind, row, partner, g_send, g_recv))
-        copies.append(hand_on(kind, row, twin, h_send, h_recv))
-
-    arrived(tr.at[1], t_recv)
-    for slot, device in ((2, down), (0, up)):
-        copy = pltpu.make_async_remote_copy(
-            src_ref=tr.at[1], dst_ref=tr.at[slot],
-            send_sem=f_send.at[slot // 2], recv_sem=f_recv.at[slot // 2],
-            device_id=device, device_id_type=MESH,
-        )
-        copy.start()
-        copies.append(copy)
 
     def send_rest(step, counts):
         v_count, e_count = counts
@@ -260,10 +231,30 @@
 
     v_count, e_count = lax.fori_loop(0, 16, send_rest, (0, 0))
 
+    copies = []
+    row_mine = 4 * source_row(p_me, core)
+    row_partner = 4 * source_row(1 - p_me, core)
     for kind in range(3):
-        row = source_row(1 - p_me, core)
-        arrived(part(kind, row), g_recv.at[kind])
-        copies.append(hand_on(kind, row, twin, i_send, i_recv))
+        for step in (0, 1, 3, 2):
+            column = (chip + step) % 4
+            ref = part(kind, row_mine + column, 1)
+            arrived(ref, o_recv.at[kind, column])
+            copies.append(hand_on(ref, partner, g_send.at[kind], g_recv.at[kind]))
+        ref = part(kind, row_mine)
+        copies.append(hand_on(ref, twin, h_send.at[kind], h_recv.at[kind]))
+
+    for step in (0, 1, 3, 2):
+        row = (chip // 4 + step) % 4
+        group = pl.ds(4 * row, 4)
+        arrived(tr.at[1, group], t_recv.at[row])
+        for slot, device in ((2, down), (0, up)):
+            copy = pltpu.make_async_remote_copy(
+                src_ref=tr.at[1, group], dst_ref=tr.at[slot, group],
+                send_sem=f_send.at[slot // 2], recv_sem=f_recv.at[slot // 2],
+                device_id=device, device_id_type=MESH,
+            )
+            copy.start()
+            copies.append(copy)
 
     def joined(low, high, row, factor):
         both = jnp.concatenate([low[row : row + ROWS], high[row : row + ROWS]], axis=0)
@@ -273,7 +264,7 @@
         return pl.ds(pl.multiple_of(q * 2 * ROWS, 16), 2 * ROWS)
 
     def flag(ref, block, entry):
-        return ref[(block + 64) % 64, entry].astype(f32)
+        return ref[entry, (block + 64) % 64].astype(f32)
 
     def shifted(ref, odd, rows):
         full = ref.astype(f32)
@@ -294,6 +285,11 @@
 
     spread_t(1)
 
+    for kind in range(3):
+        ref = part(kind, row_partner)
+        arrived(ref, g_recv.at[kind])
+        copies.append(hand_on(ref, twin, i_send.at[kind], i_recv.at[kind]))
+
     arrived(vr, v_recv)
     v_factors = [flag(vm_ref, s_me, g) for g in range(3)]
 
@@ -305,48 +301,6 @@
         return carry
 
     lax.fori_loop(0, 8, spread_v, 0)
-
-    arrived(er, e_recv)
-    edge_block = jnp.where(core == 0, s_me - 3, s_me + 3)
-    edge_factor = jnp.where(core == 0, flag(om_ref, edge_block, 2), flag(om_ref, edge_block, 0))
-
-    def spread_e(q, carry):
-        low, high = er[2 * q].astype(f32), er[2 * q + 1].astype(f32)
-
-        @pl.when(core == 0)
-        def _():
-            col[0, window(q), :] = joined(low, high, 8, edge_factor)
-
-        @pl.when(core == 1)
-        def _():
-            at = pl.ds(pl.multiple_of(2 * BLK + q * 2 * ROWS, 16), 2 * ROWS)
-            col[5, at, :] = joined(low, high, 0, edge_factor)
-
-        return carry
-
-    lax.fori_loop(0, 8, spread_e, 0)
-
-    for kind in range(3):
-        arrived(part(kind, source_row(p_me, 1 - core)), h_recv.at[kind])
-        arrived(part(kind, source_row(1 - p_me, 1 - core)), i_recv.at[kind])
-        first, rows = O_SPAN[kind]
-        wanted = [
-            (k, g, 2 * kind + k + g - 1)
-            for k in range(2) for g in range(3)
-            if 0 <= 2 * kind + k + g - 1 < 6
-        ]
-        base = 16 * z + 2 * (j_me + kind - 1)
-        factors = [flag(om_ref, base + k, g) for k, g, _ in wanted]
-
-        def spread_o(q, carry):
-            low = oc[kind, 2 * q, first : first + rows].astype(f32)
-            high = oc[kind, 2 * q + 1, first : first + rows].astype(f32)
-            for (k, g, column), factor in zip(wanted, factors):
-                at = pl.ds(pl.multiple_of((2 - g) * BLK + q * 2 * ROWS, 16), 2 * ROWS)
-                col[column, at, :] = joined(low, high, (3 * k + g) * ROWS - first, factor)
-            return carry
-
-        lax.fori_loop(0, 8, spread_o, 0)
 
     for slot in (0, 2):
         arrived(tr.at[slot], f_recv.at[slot // 2])
@@ -362,6 +316,48 @@
                 )
                 total = term if total is None else total + term
         w[:, o * BLK : (o + 1) * BLK] = total.astype(bf)
+    arrived(er, e_recv)
+    edge_block = jnp.where(core == 0, s_me - 3, s_me + 3)
+    edge_factor = jnp.where(core == 0, flag(om_ref, edge_block, 2), flag(om_ref, edge_block, 0))
+
+    def spread_e(q, carry):
+        low, high = er[2 * q].astype(f32), er[2 * q + 1].astype(f32)
+
+        @pl.when(core == 0)
+        def _():
+            col[0, window(q), :] = joined(low, high, 8, edge_factor)
+
+        @pl.when(core == 1)
+        def _():
+            at = pl.ds(pl.multiple_of(2 * BLK + q * 2 * ROWS, 16), 2 * ROWS)
+            col[5, at, :] = joined(low, high, 0, edge_factor)
+
+        return carry
+
+    lax.fori_loop(0, 8, spread_e, 0)
+
+    for kind in range(3):
+        arrived(part(kind, 4 * source_row(p_me, 1 - core)), h_recv.at[kind])
+        arrived(part(kind, 4 * source_row(1 - p_me, 1 - core)), i_recv.at[kind])
+        first, rows = O_SPAN[kind]
+        wanted = [
+            (k, g, 2 * kind + k + g - 1)
+            for k in range(2) for g in range(3)
+            if 0 <= 2 * kind + k + g - 1 < 6
+        ]
+        base = 16 * z + 2 * (j_me + kind - 1)
+        factors = [flag(om_ref, base + k, g) for k, g, _ in wanted]
+
+        def spread_o(q, carry):
+            low = oc[kind, 2 * q, first : first + rows].astype(f32)
+            high = oc[kind, 2 * q + 1, first : first + rows].astype(f32)
+            for (k, g, column), factor in zip(wanted, factors):
+                at = pl.ds(pl.multiple_of((2 - g) * BLK + q * 2 * ROWS, 16), 2 * ROWS)
+                col[column, at, :] = joined(low, high, (3 * k + g) * ROWS - first, factor)
+            return carry
+
+        lax.fori_loop(0, 8, spread_o, 0)
+
     for h in range(HB):
         block = jnp.dot(
             w[:, h * BLK : (h + 3) * BLK], col[core + h], preferred_element_type=f32
@@ -401,7 +397,9 @@
         ts = [t_loc[q, pair].astype(f32) for q in range(2)]
         for p in range(2):
             for half in range(2):
-                y = y_ref[p, 2 * pair + half].astype(f32)[: HB * ROWS]
+                y = y_ref[p, 2 * pair + half][: HB * ROWS]
+                out_ref[p, 2 * pair + half] = y
+                y = y.astype(f32)
                 for q in range(2):
                     both = y * ts[q][half * HB * ROWS : (half + 1) * HB * ROWS]
                     both = jnp.sum(both.reshape(HB * ROWS // 8, 8, BLK), axis=0)
@@ -409,12 +407,13 @@
         return tuple(sums)
 
     sums = lax.fori_loop(0, 4, couple, (jnp.zeros((8, BLK), f32),) * 4)
+    row = lax.broadcasted_iota(jnp.int32, (8, 128), 0)
     lane = lax.broadcasted_iota(jnp.int32, (8, 128), 1)
     mine = jnp.zeros((8, 128), f32)
     for k in range(4):
         part_sum = sums[k][:, :128] + sums[k][:, 128:256] + sums[k][:, 256:]
-        column = jnp.sum(part_sum, axis=1, keepdims=True)
-        mine = mine + jnp.where(lane == k, column, 0.0)
+        part_sum = jnp.sum(jnp.sum(part_sum, axis=0, keepdims=True), axis=1, keepdims=True)
+        mine = mine + jnp.where((row == k // 2) & (lane == k % 2), part_sum, 0.0)
     held[0] = mine
     slots[chip] = mine
 
@@ -447,8 +446,7 @@
     total = slots2[0]
     for k in range(1, 8):
         total = total + slots2[k]
-    total = jnp.sum(total, axis=0, keepdims=True)
-    c_ref[...] = jnp.broadcast_to(total, (8, 128)) / math.sqrt(BASIS * HB * BLK)
+    c_ref[...] = total[:2, :2] / math.sqrt(BASIS * HB * BLK)
     arrived(most, s_send)
     arrived(most2, s_send2)
     drain(y_count, y_send.at[0], y_out)
@@ -463,12 +461,13 @@
     product, coupling = pl.pallas_call(
         rpa_kernel,
         out_shape=(
-            jax.ShapeDtypeStruct((2, 8, T_ROWS, BLK), bf),
-            jax.ShapeDtypeStruct((8, 128), f32),
+            jax.ShapeDtypeStruct((2, 8, HB * ROWS, BLK), bf),
+            jax.ShapeDtypeStruct((2, 2), f32),
         ),
         in_specs=[smem] * 3 + [anywhere] * 3,
         out_specs=(vmem, vmem),
         scratch_shapes=[
+            pltpu.VMEM((2, 8, T_ROWS, BLK), bf),
             pltpu.VMEM((3, 16, T_ROWS, BLK), bf),
             pltpu.VMEM((16, V_ROWS, BLK), bf),
             pltpu.VMEM((3, 16, O_ROWS, BLK), bf),
@@ -483,7 +482,7 @@
             pltpu.VMEM((16, 8, 128), f32),
             pltpu.VMEM((2, 8, 128), f32),
             pltpu.VMEM((8, 8, 128), f32),
-            dma, dma, dma, dma, dma, dma((3,)), dma((3,)), dma, dma,
+            dma, dma, dma((4,)), dma, dma, dma((3,)), dma((3, 4)), dma, dma,
             dma((2,)), dma((2,)), dma((3,)), dma((3,)), dma((3,)), dma((3,)), dma((3,)), dma((3,)),
             dma, dma, dma, dma, dma, dma,
         ],
@@ -495,13 +494,12 @@
         ),
         name="rpa_point",
     )(
-        tensor_mask, occupied_mask, virtual_mask,
+        tensor_mask.T, occupied_mask.T, virtual_mask.T,
         tensor.reshape(2, 4, 2 * HB * ROWS, BLK),
         virtual.reshape(4, O_ROWS, BLK),
         occupied.reshape(4, O_ROWS, BLK),
     )
-    rows = product[:, :, : HB * ROWS].reshape(2, 8, HB, ROWS, BLK)
-    return (rows, coupling[0, :4].reshape(2, 2))
+    return (product.reshape(2, 8, HB, ROWS, BLK), coupling)
 
 
 def solution(mesh):

time: 130 us -> 119 us (0.915)
  Pallas kernels: 121 us -> 115 us
  local copies, waits for them, and re-layouts: 8.1 us -> 3.2 us
    pallas_call x1, Pallas kernels: 121 us -> 115 us  [shards(): pl.pallas_call(rpa_kernel, out_shape=(jax.ShapeDtypeStruct((2, 8, HB * RO...]
    slice x2 -> x0, local copies, waits for them, and re-layouts: 3.33 us -> none  [the longest x1 2.64 us: shards(): rows = product[:, :, :HB * ROWS].reshape(2, 8, HB, ROWS, BLK)]
    unnamed x3 -> x4, local copies, waits for them, and re-layouts: 4.12 us -> 3.2 us
where the time goes in v1:
time: 119 us
  Pallas kernels  115 us (97%)
  local copies, waits for them, and re-layouts  3.2 us (3%)
    pallas_call x1, Pallas kernels, shards(): pl.pallas_call(rpa_kernel, out_shape=(jax.ShapeDtypeStruct((2, 8, HB * RO...  115 us
    unnamed x4, local copies, waits for them, and re-layouts  3.2 us

profile of v1, /device:TPU:1, one launch (start us, length us, event | category | flops | bytes accessed | tf_op | source)
XLA Modules:
  0.0 119.0 jit_solution(4793302878691907308)
XLA Ops:
  0.6 115.2 %rpa_point.1 = (bf16[2,8,120,384]{3,2,1,0:T(8,128)(2,1)}, f32[2,2]{1,0:T(2,128)}) custom-call(s32[5,64]{1,0:T(8,128)} %bitcast.11, s32[3,64]{1,0:T(4,128)} %bitcast.12, s32[3,64]{1,0:T(4,128)} %bitcast.13, bf16[2,4,240,384]{3,2,1,0:T(8,128)(2,1)} %bitcast.8, bf16[4,144,384]{2,1,0:T(8,128)(2,1)} %bitcast.9, bf16[4,144,384]{2,1,0:T(8,128)(2,1)} %bitcast.10), custom_call_target="tpu_custom_call" | custom-call | flops 3397386240 | bytes 20000000 | tf_op jit(solution)/shard_map/rpa_point/pallas_call | solution.py:461
  115.8 0.0 copy-start
  115.8 2.6 %copy.10 = bf16[2,8,5,24,384]{4,3,2,1,0:T(8,128)(2,1)} copy(bf16[2,8,5,24,384]{4,3,2,1,0:T(8,128)(2,1)} %bitcast.7) | data formatting | bytes 2949120
  118.5 0.0 copy-done
  118.5 0.6 copy.11
Async XLA Ops:
  115.8 2.6 %copy-start = (f32[2,2]{1,0:T(2,128)S(1)}, f32[2,2]{1,0:T(2,128)}, u32[]{:S(2)}) copy-start(f32[2,2]{1,0:T(2,128)} %get-tuple-element.9) | copy-start | bytes 52

commit v2 on v1

--- a/solution.py
+++ b/solution.py
@@ -102,10 +102,10 @@
 
 def rpa_kernel(
     tm_ref, om_ref, vm_ref, t_ref, v_ref, o_ref, out_ref, c_ref,
-    y_ref, tr, vr, oc, er, t_loc, tc, vv, col, w, prod, y_send, slots, held, slots2,
+    y_ref, tr, vr, oc, er, t_loc, tc, vv, col, acc, w, prod, y_send, slots, held, slots2,
     loc_sem, t_send, t_recv, v_send, v_recv, o_send, o_recv, e_send, e_recv,
     f_send, f_recv, h_send, h_recv, g_send, g_recv, i_send, i_recv,
-    y_out, y_in, s_send, s_recv, s_send2, s_recv2,
+    y_out, y_in, s_send, s_recv, s_send2, s_recv2, k_send, k_recv,
 ):
     f32, bf = jnp.float32, jnp.bfloat16
     a, chip, z, core = place()
@@ -171,8 +171,6 @@
                 )
         return tuple(counts)
 
-    o_counts = lax.fori_loop(0, 16, send_occ, (0, 0, 0))
-
     def send_t(step, count):
         chip_to = target_chip(step, chip, core)
         p, j = work_of(chip_to)
@@ -186,8 +184,6 @@
             )
         return count
 
-    t_count = lax.fori_loop(0, 16, send_t, 0)
-
     def part(kind, start, count=4):
         first, rows = O_SPAN[kind]
         return oc.at[kind, pl.ds(start, count), pl.ds(first, rows)]
@@ -203,8 +199,8 @@
     def arrived(ref, sem):
         pltpu.make_async_copy(ref, ref, sem).wait()
 
-    def send_rest(step, counts):
-        v_count, e_count = counts
+    def send_v(step, counts):
+        v_count = counts
         chip_to = target_chip(step, chip, core)
         p, j = work_of(chip_to)
         same = chip_to == chip
@@ -212,28 +208,42 @@
         pair = jnp.where(mine, j - 4 * core, 0)
         for half in range(2):
             v_count = v_count + send(
-                mine, same & (core == half),
-                v_ref.at[pair, pl.ds(64 * half, V_ROWS)], vr.at[chip], v_send, v_recv,
+                mine & (p == p_want), same & (core == half),
+                v_ref.at[pair, pl.ds(64 * half, V_ROWS)], vr.at[chip],
+                v_send, v_recv.at[chip // 4],
                 (2 * z + half, chip_to),
             )
+        return v_count
+
+    def send_e(step, counts):
+        e_count = counts
+        chip_to = target_chip(step, chip, core)
+        p, j = work_of(chip_to)
+        same = chip_to == chip
         for j_rel, to_z, inside in planes(j):
             for to_core, first, kind in ((0, 112, -2), (1, 0, 2)):
                 ml = j_rel + kind - 4 * core
-                hit = (ml >= 0) & (ml < 4)
+                hit = (ml >= 0) & (ml < 4) & (p == p_want)
                 ml = jnp.where(hit, ml, 0)
                 own = same & (core == to_core)
                 e_count = e_count + send(
                     hit, own if inside else (own & False),
-                    o_ref.at[ml, pl.ds(first, E_ROWS)], er.at[chip], e_send, e_recv,
+                    o_ref.at[ml, pl.ds(first, E_ROWS)], er.at[chip],
+                    e_send, e_recv.at[chip // 4],
                     (2 * to_z + to_core, chip_to),
                 )
-        return v_count, e_count
-
-    v_count, e_count = lax.fori_loop(0, 16, send_rest, (0, 0))
+        return e_count
+
+    def pair_of_rows(p):
+        return jnp.where(p == 0, 0, 1), jnp.where(p == 0, 3, 2)
 
     copies = []
     row_mine = 4 * source_row(p_me, core)
     row_partner = 4 * source_row(1 - p_me, core)
+    t_count = lax.fori_loop(0, 16, send_t, 0)
+    o_counts = lax.fori_loop(0, 16, send_occ, (0, 0, 0))
+    v_count = lax.fori_loop(0, 16, send_v, 0)
+    e_count = lax.fori_loop(0, 16, send_e, 0)
     for kind in range(3):
         for step in (0, 1, 3, 2):
             column = (chip + step) % 4
@@ -256,6 +266,22 @@
             copy.start()
             copies.append(copy)
 
+    for ref, rows_in, send_sem, recv_sem in (
+        (vr, v_recv, k_send.at[0], k_recv.at[0]),
+    ):
+        for row in pair_of_rows(p_me):
+            group = ref.at[pl.ds(4 * row, 4)]
+            arrived(group, rows_in.at[row])
+            copies.append(hand_on(group, partner, send_sem, recv_sem))
+
+    for ref, rows_in, send_sem, recv_sem in (
+        (er, e_recv, k_send.at[1], k_recv.at[1]),
+    ):
+        for row in pair_of_rows(p_me):
+            group = ref.at[pl.ds(4 * row, 4)]
+            arrived(group, rows_in.at[row])
+            copies.append(hand_on(group, partner, send_sem, recv_sem))
+
     def joined(low, high, row, factor):
         both = jnp.concatenate([low[row : row + ROWS], high[row : row + ROWS]], axis=0)
         return (both * factor).astype(bf)
@@ -290,7 +316,7 @@
         arrived(ref, g_recv.at[kind])
         copies.append(hand_on(ref, twin, i_send.at[kind], i_recv.at[kind]))
 
-    arrived(vr, v_recv)
+    arrived(vr.at[pl.ds(0, 8)], k_recv.at[0])
     v_factors = [flag(vm_ref, s_me, g) for g in range(3)]
 
     def spread_v(q, carry):
@@ -302,21 +328,36 @@
 
     lax.fori_loop(0, 8, spread_v, 0)
 
-    for slot in (0, 2):
-        arrived(tr.at[slot], f_recv.at[slot // 2])
-        spread_t(slot)
-
-    for o in range(7):
-        total = None
-        for g in range(3):
-            h = o - g
-            if 0 <= h < HB:
-                term = jnp.dot(
-                    vv[g], tc[g, :, h * BLK : (h + 1) * BLK], preferred_element_type=f32
-                )
-                total = term if total is None else total + term
-        w[:, o * BLK : (o + 1) * BLK] = total.astype(bf)
-    arrived(er, e_recv)
+    def term(g, o):
+        h = o - g
+        return jnp.dot(vv[g], tc[g, :, h * BLK : (h + 1) * BLK], preferred_element_type=f32)
+
+    for o in range(1, 6):
+        acc[o] = term(1, o)
+
+    def neighbours(near, far):
+        arrived(tr.at[near], f_recv.at[near // 2])
+        spread_t(near)
+        for o in range(near, near + HB):
+            value = term(near, o)
+            acc[o] = acc[o] + value if 1 <= o <= 5 else value
+        arrived(tr.at[far], f_recv.at[far // 2])
+        spread_t(far)
+        for o in range(7):
+            value = term(far, o) if far <= o < far + HB else None
+            if 1 <= o <= 5 or near <= o < near + HB:
+                value = acc[o] if value is None else acc[o] + value
+            w[:, o * BLK : (o + 1) * BLK] = value.astype(bf)
+
+    @pl.when(core == 0)
+    def _():
+        neighbours(2, 0)
+
+    @pl.when(core == 1)
+    def _():
+        neighbours(0, 2)
+
+    arrived(er.at[pl.ds(0, 8)], k_recv.at[1])
     edge_block = jnp.where(core == 0, s_me - 3, s_me + 3)
     edge_factor = jnp.where(core == 0, flag(om_ref, edge_block, 2), flag(om_ref, edge_block, 0))
 
@@ -336,7 +377,7 @@
 
     lax.fori_loop(0, 8, spread_e, 0)
 
-    for kind in range(3):
+    def spread_kind(kind):
         arrived(part(kind, 4 * source_row(p_me, 1 - core)), h_recv.at[kind])
         arrived(part(kind, 4 * source_row(1 - p_me, 1 - core)), i_recv.at[kind])
         first, rows = O_SPAN[kind]
@@ -358,28 +399,37 @@
 
         lax.fori_loop(0, 8, spread_o, 0)
 
-    for h in range(HB):
-        block = jnp.dot(
-            w[:, h * BLK : (h + 3) * BLK], col[core + h], preferred_element_type=f32
-        )
-        prod[h] = block * flag(tm_ref, s_me, h)
-
     to_core = j_me // 4
     il_me = 2 * (j_me % 4) + core
 
-    def regroup(step, count):
-        chip_to = target_chip(step, chip, core)
-        rows = pl.ds(pl.multiple_of(chip_to * ROWS, 8), ROWS)
-        pieces = [prod[h, rows, :] for h in range(HB)]
-        pieces.append(jnp.zeros((T_ROWS - HB * ROWS, BLK), f32))
-        y_send[chip_to] = jnp.concatenate(pieces, axis=0).astype(bf)
-        return count + send(
-            chip_to >= 0, (chip_to == chip) & (to_core == core),
-            y_send.at[chip_to], y_ref.at[p_me, il_me], y_out, y_in,
-            (2 * z + to_core, chip_to),
-        )
-
-    y_count = lax.fori_loop(0, 16, regroup, 0)
+    def finish(blocks, first, rows, index):
+        for h in blocks:
+            block = jnp.dot(
+                w[:, h * BLK : (h + 3) * BLK], col[core + h], preferred_element_type=f32
+            )
+            prod[h] = block * flag(tm_ref, s_me, h)
+
+        def regroup(step, count):
+            chip_to = target_chip(step, chip, core)
+            at = pl.ds(pl.multiple_of(chip_to * ROWS, 8), ROWS)
+            pieces = [prod[h, at, :] for h in blocks]
+            if rows > len(blocks) * ROWS:
+                pieces.append(jnp.zeros((rows - len(blocks) * ROWS, BLK), f32))
+            window_to = pl.ds(first, rows)
+            y_send[chip_to, window_to] = jnp.concatenate(pieces, axis=0).astype(bf)
+            return count + send(
+                chip_to >= 0, (chip_to == chip) & (to_core == core),
+                y_send.at[chip_to, window_to], y_ref.at[p_me, il_me, window_to],
+                y_out.at[index], y_in.at[index], (2 * z + to_core, chip_to),
+            )
+
+        return lax.fori_loop(0, 16, regroup, 0)
+
+    spread_kind(0)
+    spread_kind(1)
+    y_count = finish((0, 1), 0, 48, 0)
+    spread_kind(2)
+    finish((2, 3, 4), 48, 80, 1)
 
     for copy in copies:
         copy.wait_send()
@@ -390,7 +440,8 @@
         drain(count, o_ref.at[0, pl.ds(0, O_SPAN[kind][1])], o_send.at[kind])
     t_copy.wait()
 
-    arrived(y_ref, y_in)
+    for index, (first, rows) in enumerate(((0, 48), (48, 80))):
+        arrived(y_ref.at[:, :, pl.ds(first, rows)], y_in.at[index])
 
     def couple(pair, sums):
         sums = list(sums)
@@ -449,7 +500,8 @@
     c_ref[...] = total[:2, :2] / math.sqrt(BASIS * HB * BLK)
     arrived(most, s_send)
     arrived(most2, s_send2)
-    drain(y_count, y_send.at[0], y_out)
+    drain(y_count, y_send.at[0, pl.ds(0, 48)], y_out.at[0])
+    drain(y_count, y_send.at[0, pl.ds(48, 80)], y_out.at[1])
 
 
 def shards(tensor, occupied, virtual, tensor_mask, occupied_mask, virtual_mask):
@@ -476,15 +528,16 @@
             pltpu.VMEM((3, BLK, HB * BLK), bf),
             pltpu.VMEM((3, BLK, BLK), bf),
             pltpu.VMEM((6, 3 * BLK, BLK), bf),
+            pltpu.VMEM((7, BLK, BLK), f32),
             pltpu.VMEM((BLK, 7 * BLK), bf),
             pltpu.VMEM((HB, BLK, BLK), f32),
             pltpu.VMEM((16, T_ROWS, BLK), bf),
             pltpu.VMEM((16, 8, 128), f32),
             pltpu.VMEM((2, 8, 128), f32),
             pltpu.VMEM((8, 8, 128), f32),
-            dma, dma, dma((4,)), dma, dma, dma((3,)), dma((3, 4)), dma, dma,
+            dma, dma, dma((4,)), dma, dma((4,)), dma((3,)), dma((3, 4)), dma, dma((4,)),
             dma((2,)), dma((2,)), dma((3,)), dma((3,)), dma((3,)), dma((3,)), dma((3,)), dma((3,)),
-            dma, dma, dma, dma, dma, dma,
+            dma((2,)), dma((2,)), dma, dma, dma, dma, dma((2,)), dma((2,)),
         ],
         compiler_params=pltpu.CompilerParams(
             collective_id=0, has_side_effects=True, vmem_limit_bytes=VMEM_LIMIT

time: 119 us -> 115 us (0.966)
  Pallas kernels: 115 us -> 111 us
    pallas_call x1, Pallas kernels: 115 us -> 111 us  [shards(): pl.pallas_call(rpa_kernel, out_shape=(jax.ShapeDtypeStruct((2, 8, HB * RO...]
where the time goes in v2:
time: 115 us
  Pallas kernels  111 us (97%)
  local copies, waits for them, and re-layouts  3.2 us (3%)
    pallas_call x1, Pallas kernels, shards(): pl.pallas_call(rpa_kernel, out_shape=(jax.ShapeDtypeStruct((2, 8, HB * RO...  111 us
    unnamed x4, local copies, waits for them, and re-layouts  3.2 us

profile of v2, /device:TPU:1, one launch (start us, length us, event | category | flops | bytes accessed | tf_op | source)
XLA Modules:
  0.0 114.6 jit_solution(11670787958379523584)
XLA Ops:
  0.6 110.8 %rpa_point.1 = (bf16[2,8,120,384]{3,2,1,0:T(8,128)(2,1)}, f32[2,2]{1,0:T(2,128)}) custom-call(s32[5,64]{1,0:T(8,128)} %bitcast.11, s32[3,64]{1,0:T(4,128)} %bitcast.12, s32[3,64]{1,0:T(4,128)} %bitcast.13, bf16[2,4,240,384]{3,2,1,0:T(8,128)(2,1)} %bitcast.8, bf16[4,144,384]{2,1,0:T(8,128)(2,1)} %bitcast.9, bf16[4,144,384]{2,1,0:T(8,128)(2,1)} %bitcast.10), custom_call_target="tpu_custom_call" | custom-call | flops 3397386240 | bytes 20000000 | tf_op jit(solution)/shard_map/rpa_point/pallas_call | solution.py:513
  111.4 0.0 copy-start
  111.4 2.6 %copy.10 = bf16[2,8,5,24,384]{4,3,2,1,0:T(8,128)(2,1)} copy(bf16[2,8,5,24,384]{4,3,2,1,0:T(8,128)(2,1)} %bitcast.7) | data formatting | bytes 2949120
  114.0 0.0 copy-done
  114.0 0.6 copy.11
Async XLA Ops:
  111.4 2.6 %copy-start = (f32[2,2]{1,0:T(2,128)S(1)}, f32[2,2]{1,0:T(2,128)}, u32[]{:S(2)}) copy-start(f32[2,2]{1,0:T(2,128)} %get-tuple-element.9) | copy-start | bytes 52

commit v3 on v2

--- a/solution.py
+++ b/solution.py
@@ -20,9 +20,21 @@
 E_ROWS = 32
 O_SPAN = ((16, 128), (0, 144), (0, 128))
 
-ORDER = (
+T_ORDER = (
+    (0, 0), (2, 2), (0, 1), (1, 0), (0, 3), (3, 0), (1, 1), (3, 2),
+    (3, 1), (1, 3), (0, 2), (2, 0), (1, 2), (2, 1), (3, 3), (2, 3),
+)
+O_ORDER = (
     (0, 0), (2, 2), (1, 0), (0, 1), (3, 0), (0, 3), (1, 1), (3, 3),
     (1, 3), (3, 1), (2, 0), (0, 2), (2, 1), (1, 2), (2, 3), (3, 2),
+)
+V_ORDER = (
+    (0, 0), (2, 2), (1, 0), (0, 1), (3, 0), (0, 3), (1, 1), (3, 3),
+    (1, 3), (3, 1), (2, 0), (0, 2), (2, 1), (1, 2), (2, 3), (3, 2),
+)
+Y_ORDER = (
+    (0, 0), (2, 2), (3, 0), (0, 3), (1, 0), (0, 1), (3, 3), (1, 1),
+    (3, 1), (1, 3), (2, 0), (0, 2), (2, 3), (3, 2), (2, 1), (1, 2),
 )
 
 
@@ -48,8 +60,8 @@
     return p, j
 
 
-def target_chip(step, chip, core):
-    dx, dy = pick([d[0] for d in ORDER], step), pick([d[1] for d in ORDER], step)
+def target_chip(order, step, chip, core):
+    dx, dy = pick([d[0] for d in order], step), pick([d[1] for d in order], step)
     ex = jnp.where(core == 0, dx, dy)
     ey = jnp.where(core == 0, dy, dx)
     return ((chip // 4 + ey) % 4) * 4 + (chip % 4 + ex) % 4
@@ -151,28 +163,30 @@
         outer_z = jnp.where(core == 0, (z + 3) % 4, (z + 1) % 4)
         return ((j, z, True), (j + jnp.where(core == 0, -8, 8), outer_z, False))
 
-    def send_occ(step, counts):
-        counts = list(counts)
-        chip_to = target_chip(step, chip, core)
-        p, j = work_of(chip_to)
-        for j_rel, to_z, inside in planes(j):
-            for kind in range(3):
-                first, rows = O_SPAN[kind]
+    def send_occ(kind):
+        first, rows = O_SPAN[kind]
+
+        def one(step, count):
+            chip_to = target_chip(O_ORDER, step, chip, core)
+            p, j = work_of(chip_to)
+            own = (chip_to == chip) & (core == core_want)
+            for j_rel, to_z, inside in planes(j):
                 ml = j_rel + kind - 1 - 4 * core
                 hit = (ml >= 0) & (ml < 4) & (p == p_want)
                 ml = jnp.where(hit, ml, 0)
-                own = (chip_to == chip) & (core == core_want)
-                counts[kind] = counts[kind] + send(
+                count = count + send(
                     hit, own if inside else (own & False),
                     o_ref.at[ml, pl.ds(first, rows)],
                     oc.at[kind, chip, pl.ds(first, rows)],
                     o_send.at[kind], o_recv.at[kind, chip % 4],
                     (2 * to_z + core_want, chip_to),
                 )
-        return tuple(counts)
+            return count
+
+        return lax.fori_loop(0, 16, one, 0)
 
     def send_t(step, count):
-        chip_to = target_chip(step, chip, core)
+        chip_to = target_chip(T_ORDER, step, chip, core)
         p, j = work_of(chip_to)
         mine = j // 4 == core
         pair = jnp.where(mine, j - 4 * core, 0)
@@ -201,7 +215,7 @@
 
     def send_v(step, counts):
         v_count = counts
-        chip_to = target_chip(step, chip, core)
+        chip_to = target_chip(V_ORDER, step, chip, core)
         p, j = work_of(chip_to)
         same = chip_to == chip
         mine = j // 4 == core
@@ -217,7 +231,7 @@
 
     def send_e(step, counts):
         e_count = counts
-        chip_to = target_chip(step, chip, core)
+        chip_to = target_chip(V_ORDER, step, chip, core)
         p, j = work_of(chip_to)
         same = chip_to == chip
         for j_rel, to_z, inside in planes(j):
@@ -241,8 +255,9 @@
     row_mine = 4 * source_row(p_me, core)
     row_partner = 4 * source_row(1 - p_me, core)
     t_count = lax.fori_loop(0, 16, send_t, 0)
-    o_counts = lax.fori_loop(0, 16, send_occ, (0, 0, 0))
+    o_counts = [send_occ(kind) for kind in (0, 1)]
     v_count = lax.fori_loop(0, 16, send_v, 0)
+    o_counts.append(send_occ(2))
     e_count = lax.fori_loop(0, 16, send_e, 0)
     for kind in range(3):
         for step in (0, 1, 3, 2):
@@ -410,7 +425,7 @@
             prod[h] = block * flag(tm_ref, s_me, h)
 
         def regroup(step, count):
-            chip_to = target_chip(step, chip, core)
+            chip_to = target_chip(Y_ORDER, step, chip, core)
             at = pl.ds(pl.multiple_of(chip_to * ROWS, 8), ROWS)
             pieces = [prod[h, at, :] for h in blocks]
             if rows > len(blocks) * ROWS:

time: 115 us -> 110 us (0.957)
  Pallas kernels: 111 us -> 106 us
    pallas_call x1, Pallas kernels: 111 us -> 106 us  [shards(): pl.pallas_call(rpa_kernel, out_shape=(jax.ShapeDtypeStruct((2, 8, HB * RO...]
where the time goes in v3:
time: 110 us
  Pallas kernels  106 us (96%)
  local copies, waits for them, and re-layouts  3.2 us (3%)
    pallas_call x1, Pallas kernels, shards(): pl.pallas_call(rpa_kernel, out_shape=(jax.ShapeDtypeStruct((2, 8, HB * RO...  106 us
    unnamed x4, local copies, waits for them, and re-layouts  3.2 us

profile of v3, /device:TPU:1, one launch (start us, length us, event | category | flops | bytes accessed | tf_op | source)
XLA Modules:
  0.0 110.0 jit_solution(4441934192846698025)
XLA Ops:
  0.6 106.2 %rpa_point.1 = (bf16[2,8,120,384]{3,2,1,0:T(8,128)(2,1)}, f32[2,2]{1,0:T(2,128)}) custom-call(s32[5,64]{1,0:T(8,128)} %bitcast.11, s32[3,64]{1,0:T(4,128)} %bitcast.12, s32[3,64]{1,0:T(4,128)} %bitcast.13, bf16[2,4,240,384]{3,2,1,0:T(8,128)(2,1)} %bitcast.8, bf16[4,144,384]{2,1,0:T(8,128)(2,1)} %bitcast.9, bf16[4,144,384]{2,1,0:T(8,128)(2,1)} %bitcast.10), custom_call_target="tpu_custom_call" | custom-call | flops 3397386240 | bytes 20000000 | tf_op jit(solution)/shard_map/rpa_point/pallas_call | solution.py:528
  106.8 0.0 copy-start
  106.8 2.6 %copy.10 = bf16[2,8,5,24,384]{4,3,2,1,0:T(8,128)(2,1)} copy(bf16[2,8,5,24,384]{4,3,2,1,0:T(8,128)(2,1)} %bitcast.7) | data formatting | bytes 2949120
  109.5 0.0 copy-done
  109.5 0.6 copy.11
Async XLA Ops:
  106.8 2.6 %copy-start = (f32[2,2]{1,0:T(2,128)S(1)}, f32[2,2]{1,0:T(2,128)}, u32[]{:S(2)}) copy-start(f32[2,2]{1,0:T(2,128)} %get-tuple-element.9) | copy-start | bytes 52
